TPU v7x, 32 devices: a whole 2x2x4 slice. The times are simulated.
32 devices in a mesh: dp: 8 (over z, x), seq: 4 (over y, core).
Axes of the slice: x: 2, y: 2, z: 4, core: 2. Of those that a mesh axis runs over, the one named last changes fastest.
Arguments:
- short_in: bfloat16 [2, 32, 256, 768], P(None, 'dp', 'seq'), may hold values from -6 to 6
- long_in: bfloat16 [2, 16, 512, 768], P(None, 'dp', 'seq'), may hold values from -6 to 6
- short_cot: bfloat16 [2, 32, 256, 768], P(None, 'dp', 'seq'), may hold values from -6 to 6
- long_cot: bfloat16 [2, 16, 512, 768], P(None, 'dp', 'seq'), may hold values from -6 to 6
- short_len: int32 [2, 8, 4], P(None, 'dp'), may hold values from 0 to 256, as said below
- long_len: int32 [2, 8, 2], P(None, 'dp'), may hold values from 0 to 512, as said below
- wide_master: float32 [768, 6144], P('dp')
- down_master: float32 [3072, 768], P('dp'), may hold values from -0.109375 to 0.109375
- vector_master: float32 [768, 12], P('dp')
- wide_moment: float32 [768, 6144], P('dp'), may hold values from -256 to 256
- down_moment: float32 [3072, 768], P('dp'), may hold values from -256 to 256
- vector_moment: float32 [768, 12], P('dp'), may hold values from -256 to 256
- wide_average: float32 [768, 6144], P('dp'), may hold values from -0.21875 to 0.21875
- down_average: float32 [3072, 768], P('dp'), may hold values from -0.109375 to 0.109375
- vector_average: float32 [768, 12], P('dp'), may hold values from -6 to 6
Outputs:
- short_out: bfloat16 [2, 32, 256, 768], P(None, 'dp', 'seq')
- long_out: bfloat16 [2, 16, 512, 768], P(None, 'dp', 'seq')
- short_back: bfloat16 [2, 32, 256, 768], P(None, 'dp', 'seq')
- long_back: bfloat16 [2, 16, 512, 768], P(None, 'dp', 'seq')
- wide_grad: float32 [768, 6144], P('dp')
- down_grad: float32 [3072, 768], P('dp')
- vector_grad: float32 [768, 12], P('dp')
- wide_velocity: float32 [768, 6144], P('dp')
- down_velocity: float32 [3072, 768], P('dp')
- vector_velocity: float32 [768, 12], P('dp')
- wide_averaged: float32 [768, 6144], P('dp')
- down_averaged: float32 [3072, 768], P('dp')
- vector_averaged: float32 [768, 12], P('dp')
- wide_updated: float32 [768, 6144], P('dp')
- down_updated: float32 [3072, 768], P('dp')
- vector_updated: float32 [768, 12], P('dp')
- wide_copy: bfloat16 [768, 6144], P('dp')
- down_copy: bfloat16 [3072, 768], P('dp')
- vector_copy: bfloat16 [768, 12], P('dp')
Inputs may be any that keep to these rules, and one draw needn't show every extreme that they name: `short_len`: 0 marks an empty slot; in each micro-batch every index of dp has at least half of its slots live and one sequence of exactly 256 tokens. `long_len`: 0 marks an empty slot; in each micro-batch every index of dp has at least half of its slots live and one sequence of exactly 512 tokens.
All inputs are finite; a program needn't handle non-finite values.
Results may differ from a plain program's by a relative error of at most 0.015.
Values may be sent and summed in bfloat16 or wider, within the bound.
A program may use at most 256 MiB of HBM per device.

v0:
```python
import jax
import jax.numpy as jnp
from jax import lax
from jax.sharding import PartitionSpec as P

D = 768
HEAD_DIM = 64
FF = 3072
norm_eps = 1e-12
mask_fill = -10000.0
learning_rate = 0.0002
momentum_rate = 0.9
decay_weight = 0.0001
average_rate = 0.9


def norm_forward(inputs, gain, shift):
    centred = inputs - jnp.mean(inputs, axis=-1, keepdims=True)
    inverse = lax.rsqrt(jnp.mean(centred * centred, axis=-1, keepdims=True) + norm_eps)
    normed = centred * inverse
    return (normed * gain + shift, normed, inverse)


def norm_backward(grad_out, normed, inverse, gain):
    scaled = grad_out * gain
    grad_in = inverse * (
        scaled
        - jnp.mean(scaled, axis=-1, keepdims=True)
        - normed * jnp.mean(scaled * normed, axis=-1, keepdims=True)
    )
    return (grad_in, jnp.sum(grad_out * normed, axis=0), jnp.sum(grad_out, axis=0))


def transpose_dot(left, right):
    return jnp.einsum("ra,rb->ab", left, right, preferred_element_type=jnp.float32)


def right_dot(left, right):
    return jnp.einsum("ra,ba->rb", left, right, preferred_element_type=jnp.float32)


def weight_grads(factor_list):
    products = []
    for kind in range(4):
        left = jnp.concatenate([factors[kind][0] for factors in factor_list], axis=0)
        right = jnp.concatenate([factors[kind][1] for factors in factor_list], axis=0)
        products.append(transpose_dot(left, right))
    return products


def micro_step(tokens, cotangent, lengths, weights, spread):
    wide_w, down_w, vector_w = weights
    seq_count, local_len, model_width = tokens.shape
    row_count = seq_count * local_len
    parts_count = lax.axis_size("seq") if spread else 1
    full_len = local_len * parts_count
    head_width = model_width // parts_count
    local_heads = head_width // HEAD_DIM
    vector = vector_w.astype(jnp.float32)
    flat_rows = tokens.reshape(row_count, model_width)
    proj_bias = jnp.concatenate(
        [vector[:, 0], jnp.zeros((model_width,), jnp.float32), vector[:, 1]]
    )
    projected = (
        jnp.dot(flat_rows, wide_w[:, : 3 * model_width], preferred_element_type=jnp.float32)
        + proj_bias
    )
    stacked = projected.astype(jnp.bfloat16).reshape(seq_count, local_len, 3, model_width)
    if spread:
        headed = lax.all_to_all(stacked, "seq", split_axis=3, concat_axis=1, tiled=True)
    else:
        headed = stacked
    headed = headed.reshape(seq_count, full_len, 3, local_heads, HEAD_DIM)
    queries = headed[:, :, 0]
    key_rows = headed[:, :, 1]
    values = headed[:, :, 2]
    key_live = (jnp.arange(full_len)[None, :] < lengths[:, None])[:, None, None, :]
    score_scale = HEAD_DIM ** (-0.5)
    raw_scores = (
        jnp.einsum("bqhd,bkhd->bhqk", queries, key_rows, preferred_element_type=jnp.float32)
        * score_scale
    )
    scores = jnp.where(key_live, raw_scores, mask_fill)
    row_top = jnp.max(scores, axis=-1, keepdims=True)
    exponent = jnp.exp(scores - row_top)
    row_total = jnp.sum(exponent, axis=-1, keepdims=True)
    log_total = row_top + jnp.log(row_total)
    probs = (exponent / row_total).astype(jnp.bfloat16)
    attended = jnp.einsum("bhqk,bkhd->bqhd", probs, values, preferred_element_type=jnp.float32)
    attended = attended.astype(jnp.bfloat16).reshape(seq_count, full_len, head_width)
    if spread:
        gathered = lax.all_to_all(attended, "seq", split_axis=1, concat_axis=2, tiled=True)
    else:
        gathered = attended
    attn_rows = gathered.reshape(row_count, model_width)
    branch = (
        jnp.dot(
            attn_rows,
            wide_w[:, 3 * model_width : 4 * model_width],
            preferred_element_type=jnp.float32,
        )
        + vector[:, 2]
    )
    first, normed_one, inverse_one = norm_forward(
        flat_rows.astype(jnp.float32) + branch, vector[:, 3], vector[:, 4]
    )
    first_low = first.astype(jnp.bfloat16)
    bias_one = jnp.transpose(vector[:, 8:]).reshape(-1)
    inner_pre = (
        jnp.dot(first_low, wide_w[:, 4 * model_width :], preferred_element_type=jnp.float32)
        + bias_one
    )
    active = jax.nn.gelu(inner_pre, approximate=False).astype(jnp.bfloat16)
    branch_two = jnp.dot(active, down_w, preferred_element_type=jnp.float32) + vector[:, 5]
    result, normed_two, inverse_two = norm_forward(first + branch_two, vector[:, 6], vector[:, 7])
    output = result.astype(jnp.bfloat16).reshape(tokens.shape)
    offset = lax.axis_index("seq") * local_len if spread else 0
    position = offset + jnp.arange(local_len)
    live_rows = (position[None, :] < lengths[:, None]).astype(jnp.float32).reshape(row_count, 1)
    grad_out = cotangent.reshape(row_count, model_width).astype(jnp.float32) * live_rows
    grad_mid, grad_gain_two, grad_shift_two = norm_backward(
        grad_out, normed_two, inverse_two, vector[:, 6]
    )
    grad_mid_low = grad_mid.astype(jnp.bfloat16)
    grad_active = right_dot(grad_mid_low, down_w)
    normal_cdf = 0.5 * (1.0 + jax.scipy.special.erf(inner_pre * 0.5**0.5))
    normal_pdf = jnp.exp(-0.5 * inner_pre * inner_pre) * (2.0 * jnp.pi) ** (-0.5)
    grad_inner = (grad_active * (normal_cdf + inner_pre * normal_pdf)).astype(jnp.bfloat16)
    grad_first = grad_mid + right_dot(grad_inner, wide_w[:, 4 * model_width :])
    grad_resid, grad_gain_one, grad_shift_one = norm_backward(
        grad_first, normed_one, inverse_one, vector[:, 3]
    )
    grad_resid_low = grad_resid.astype(jnp.bfloat16)
    grad_attended = right_dot(grad_resid_low, wide_w[:, 3 * model_width : 4 * model_width])
    grad_attended = grad_attended.astype(jnp.bfloat16).reshape(seq_count, local_len, model_width)
    if spread:
        grad_headed = lax.all_to_all(grad_attended, "seq", split_axis=2, concat_axis=1, tiled=True)
    else:
        grad_headed = grad_attended
    grad_heads = grad_headed.reshape(seq_count, full_len, local_heads, HEAD_DIM)
    again_scores = jnp.where(
        key_live,
        jnp.einsum("bqhd,bkhd->bhqk", queries, key_rows, preferred_element_type=jnp.float32)
        * score_scale,
        mask_fill,
    )
    prob_exact = jnp.exp(again_scores - log_total)
    grad_probs = jnp.einsum(
        "bqhd,bkhd->bhqk", grad_heads, values, preferred_element_type=jnp.float32
    )
    grad_scores = prob_exact * (
        grad_probs - jnp.sum(prob_exact * grad_probs, axis=-1, keepdims=True)
    )
    grad_scores = jnp.where(key_live, grad_scores, 0.0).astype(jnp.bfloat16)
    grad_query = (
        jnp.einsum("bhqk,bkhd->bqhd", grad_scores, key_rows, preferred_element_type=jnp.float32)
        * score_scale
    )
    grad_key = (
        jnp.einsum("bhqk,bqhd->bkhd", grad_scores, queries, preferred_element_type=jnp.float32)
        * score_scale
    )
    grad_value = jnp.einsum(
        "bhqk,bqhd->bkhd", probs, grad_heads, preferred_element_type=jnp.float32
    )
    grad_stack = jnp.stack([grad_query, grad_key, grad_value], axis=2)
    grad_stack = grad_stack.astype(jnp.bfloat16).reshape(seq_count, full_len, 3, head_width)
    if spread:
        grad_local = lax.all_to_all(grad_stack, "seq", split_axis=1, concat_axis=3, tiled=True)
    else:
        grad_local = grad_stack
    grad_proj = grad_local.reshape(row_count, 3 * model_width)
    grad_input = grad_resid + right_dot(grad_proj, wide_w[:, : 3 * model_width])
    back = grad_input.astype(jnp.bfloat16).reshape(tokens.shape)
    proj_sums = jnp.sum(grad_proj.astype(jnp.float32), axis=0)
    grad_bias_one = jnp.sum(grad_inner.astype(jnp.float32), axis=0)
    grad_columns = jnp.stack(
        [
            proj_sums[:model_width],
            proj_sums[2 * model_width :],
            jnp.sum(grad_resid_low.astype(jnp.float32), axis=0),
            grad_gain_one,
            grad_shift_one,
            jnp.sum(grad_mid_low.astype(jnp.float32), axis=0),
            grad_gain_two,
            grad_shift_two,
        ],
        axis=1,
    )
    grad_vector = jnp.concatenate(
        [grad_columns, jnp.transpose(grad_bias_one.reshape(-1, model_width))], axis=1
    )
    factors = (
        (flat_rows, grad_proj),
        (attn_rows, grad_resid_low),
        (first_low, grad_inner),
        (active, grad_mid_low),
    )
    return (output, back, factors, grad_vector)


def update(master, reduced_grad, moment, average):
    step_grad = reduced_grad + decay_weight * master
    velocity = momentum_rate * moment + step_grad
    updated = master - learning_rate * (step_grad + momentum_rate * velocity)
    averaged = average_rate * average + (1.0 - average_rate) * updated
    return (velocity, averaged, updated, updated.astype(jnp.bfloat16))


def body(
    short_in,
    long_in,
    short_cot,
    long_cot,
    short_len,
    long_len,
    wide_master,
    down_master,
    vector_master,
    wide_moment,
    down_moment,
    vector_moment,
    wide_average,
    down_average,
    vector_average,
):
    weights = (
        lax.all_gather(wide_master.astype(jnp.bfloat16), "dp", axis=0, tiled=True),
        lax.all_gather(down_master.astype(jnp.bfloat16), "dp", axis=0, tiled=True),
        lax.all_gather(vector_master.astype(jnp.bfloat16), "dp", axis=0, tiled=True),
    )
    own_rows = wide_master.shape[0]
    sums = (
        jnp.zeros((own_rows, 3 * D), jnp.float32),
        jnp.zeros((own_rows, D), jnp.float32),
        jnp.zeros((own_rows, FF), jnp.float32),
        jnp.zeros(down_master.shape, jnp.float32),
        jnp.zeros(vector_master.shape, jnp.float32),
    )
    factor_list = []
    vector_total = jnp.zeros(weights[2].shape, jnp.float32)
    bucket_results = []
    for bucket_index, (tokens, cotangent, lengths) in enumerate(
        ((short_in, short_cot, short_len), (long_in, long_cot, long_len))
    ):
        outputs = []
        backs = []
        for micro_index in range(tokens.shape[0]):
            micro_tokens = tokens[micro_index]
            micro_cot = cotangent[micro_index]
            micro_len = lengths[micro_index, 0]
            if bucket_index == 0:
                own_count = micro_tokens.shape[0] // lax.axis_size("seq")
                whole_tokens, whole_cot = (
                    lax.all_to_all(micro_tokens, "seq", split_axis=0, concat_axis=1, tiled=True),
                    lax.all_to_all(micro_cot, "seq", split_axis=0, concat_axis=1, tiled=True),
                )
                own_len = lax.dynamic_slice_in_dim(
                    micro_len, lax.axis_index("seq") * own_count, own_count
                )
                whole_out, whole_back, factors, grad_vector = micro_step(
                    whole_tokens, whole_cot, own_len, weights, False
                )
                output, back = (
                    lax.all_to_all(whole_out, "seq", split_axis=1, concat_axis=0, tiled=True),
                    lax.all_to_all(whole_back, "seq", split_axis=1, concat_axis=0, tiled=True),
                )
            else:
                output, back, factors, grad_vector = micro_step(
                    micro_tokens, micro_cot, micro_len, weights, True
                )
            factor_list.append(factors)
            vector_total = vector_total + grad_vector
            outputs.append(output)
            backs.append(back)
        bucket_results.append((jnp.stack(outputs), jnp.stack(backs)))
    products = weight_grads(factor_list)
    sums = (
        lax.psum_scatter(products[0], "dp", scatter_dimension=0, tiled=True),
        lax.psum_scatter(products[1], "dp", scatter_dimension=0, tiled=True),
        lax.psum_scatter(products[2], "dp", scatter_dimension=0, tiled=True),
        lax.psum_scatter(products[3], "dp", scatter_dimension=0, tiled=True),
        lax.psum_scatter(vector_total, "dp", scatter_dimension=0, tiled=True),
    )
    reduced = (
        lax.psum(sums[0].astype(jnp.bfloat16), "seq").astype(jnp.float32),
        lax.psum(sums[1].astype(jnp.bfloat16), "seq").astype(jnp.float32),
        lax.psum(sums[2].astype(jnp.bfloat16), "seq").astype(jnp.float32),
        lax.psum(sums[3].astype(jnp.bfloat16), "seq").astype(jnp.float32),
        lax.psum(sums[4].astype(jnp.bfloat16), "seq").astype(jnp.float32),
    )
    wide_reduced = jnp.concatenate([reduced[0], reduced[1], reduced[2]], axis=1)
    down_reduced = reduced[3]
    vector_reduced = reduced[4]
    wide_new = update(wide_master, wide_reduced, wide_moment, wide_average)
    down_new = update(down_master, down_reduced, down_moment, down_average)
    vector_new = update(vector_master, vector_reduced, vector_moment, vector_average)
    return (
        bucket_results[0][0],
        bucket_results[1][0],
        bucket_results[0][1],
        bucket_results[1][1],
        wide_reduced,
        down_reduced,
        vector_reduced,
        wide_new[0],
        down_new[0],
        vector_new[0],
        wide_new[1],
        down_new[1],
        vector_new[1],
        wide_new[2],
        down_new[2],
        vector_new[2],
        wide_new[3],
        down_new[3],
        vector_new[3],
    )


def solution(mesh):
    return jax.shard_map(
        body,
        mesh=mesh,
        in_specs=(
            P(None, "dp", "seq", None),
            P(None, "dp", "seq", None),
            P(None, "dp", "seq", None),
            P(None, "dp", "seq", None),
            P(None, "dp", None),
            P(None, "dp", None),
            P("dp", None),
            P("dp", None),
            P("dp", None),
            P("dp", None),
            P("dp", None),
            P("dp", None),
            P("dp", None),
            P("dp", None),
            P("dp", None),
        ),
        out_specs=(
            P(None, "dp", "seq", None),
            P(None, "dp", "seq", None),
            P(None, "dp", "seq", None),
            P(None, "dp", "seq", None),
            P("dp", None),
            P("dp", None),
            P("dp", None),
            P("dp", None),
            P("dp", None),
            P("dp", None),
            P("dp", None),
            P("dp", None),
            P("dp", None),
            P("dp", None),
            P("dp", None),
            P("dp", None),
            P("dp", None),
            P("dp", None),
            P("dp", None),
        ),
        check_vma=False,
    )
```

profile of v0, /device:TPU:0, one launch (start us, length us, event | category | flops | bytes accessed | tf_op | source)
XLA Modules:
  0.0 1123.6 jit_solution(16164182160932773514)
XLA Ops:
  11.2 4.4 all-to-all-start.8
  20.8 32.3 %all-gather = bf16[8,96,12]{1,2,0:T(8,128)(2,1)S(1)} all-gather(bf16[1,96,12]{1,2,0:T(8,128)(2,1)S(1)} %convert_bitcast_fusion), channel_id=1, replica_groups=mesh['dp'=8,'seq'=4] {'dp'}, dimensions={0}, use_global_device_ids=true | all-gather | bytes 20736 | tf_op jit(solution)/shard_map/all_gather | solution.py:230
  65.1 4.7 all-to-all-done.10
  75.5 5.2 all-to-all-done.2
  84.2 67.5 %all-gather.4.cloned.1.call-done = bf16[768,6144]{1,0:T(8,128)(2,1)} async-done(((bf16[96,6144]{1,0:T(8,128)(2,1)}), bf16[768,6144]{1,0:T(8,128)(2,1)}) %all-gather.4.cloned.1.call-update) | async-done | bytes 9437200 | tf_op jit(solution)/shard_map/all_gather | solution.py:228
  160.9 5.0 copy.368
  170.9 5.0 copy.375
  175.8 4.8 all-to-all-start.4
  180.7 4.1 fusion.40
  209.6 6.8 all-to-all-done.6
  251.7 6.2 all-to-all-done.5
  266.9 10.8 fusion.66
  277.8 4.5 fusion.382
  282.6 9.5 fusion.63
  294.9 10.0 fusion.69
  306.7 9.6 fusion.60
  359.8 4.1 all-to-all-start.14
  372.6 4.0 fusion.177
  376.7 6.7 fusion.241
  383.4 6.7 fusion.247
  393.3 4.1 all-to-all-start.12
  414.6 5.0 fusion.316
  419.5 11.7 %fusion.269 = bf16[2,3,64,512]{3,2,1,0:T(8,128)(2,1)S(1)} fusion(f32[2,3,512,512]{2,3,1,0:T(8,128)} %fusion.316, f32[2,3,512,512]{2,3,1,0:T(8,128)} %copy-done.1, f32[2,3,512]{2,1,0:T(4,128)S(1)} %copy-done.104, pred[2,512]{1,0:T(4,128)(4,1)S(1)} %copy-done.85, bf16[2,512,3,3,64]{1,4,3,0,2:T(8,128)(2,1)S(1)} %copy-done.18), kind=kOutput, calls=%fused_computation.309 | convolution fusion | flops 219024896 | bytes 25989120 | tf_op jit(solution)/shard_map/bhqk,bkhd->bqhd/dot_general | solution.py:156
  431.7 11.9 %fusion.266 = bf16[2,3,64,512]{3,2,1,0:T(8,128)(2,1)S(1)} fusion(f32[2,3,512,512]{2,3,1,0:T(8,128)} %fusion.316, f32[2,3,512,512]{2,3,1,0:T(8,128)} %copy-done.1, f32[2,3,512]{2,1,0:T(4,128)S(1)} %copy-done.104, pred[2,512]{1,0:T(4,128)(4,1)S(1)} %copy-done.85, bf16[2,512,3,3,64]{1,4,3,0,2:T(8,128)(2,1)S(1)} %copy-done.18), kind=kOutput, calls=%fused_computation.308 | convolution fusion | flops 219024896 | bytes 25989120 | tf_op jit(solution)/shard_map/bhqk,bqhd->bkhd/dot_general | solution.py:160
  447.3 4.0 all-to-all-start.13
  455.0 11.6 %fusion.275 = bf16[2,3,64,512]{3,2,1,0:T(8,128)(2,1)S(1)} fusion(f32[2,3,512,512]{2,3,1,0:T(8,128)} %fusion.318, f32[2,3,512,512]{2,3,1,0:T(8,128)} %copy-done, f32[2,3,512]{2,1,0:T(4,128)} %log_add_fusion, pred[2,512]{1,0:T(4,128)(4,1)S(1)} %copy-done.83, bf16[2,512,3,3,64]{1,4,3,0,2:T(8,128)(2,1)S(1)} %copy-done.17), kind=kOutput, calls=%fused_computation.311 | convolution fusion | flops 219024896 | bytes 25989120 | tf_op jit(solution)/shard_map/bhqk,bkhd->bqhd/dot_general | solution.py:156
  467.7 11.8 %fusion.272 = bf16[2,3,64,512]{3,2,1,0:T(8,128)(2,1)S(1)} fusion(f32[2,3,512,512]{2,3,1,0:T(8,128)} %fusion.318, f32[2,3,512,512]{2,3,1,0:T(8,128)} %copy-done, f32[2,3,512]{2,1,0:T(4,128)} %log_add_fusion, pred[2,512]{1,0:T(4,128)(4,1)S(1)} %copy-done.83, bf16[2,512,3,3,64]{1,4,3,0,2:T(8,128)(2,1)S(1)} %copy-done.17), kind=kOutput, calls=%fused_computation.310 | convolution fusion | flops 219024896 | bytes 25989120 | tf_op jit(solution)/shard_map/bhqk,bqhd->bkhd/dot_general | solution.py:160
  480.6 4.9 pad_maximum_fusion.1
  485.5 4.4 all-to-all-start.15
  492.2 6.9 fusion.253
  499.1 6.9 fusion.259
  521.0 7.7 fusion.28
  528.8 9.9 fusion.4
  538.8 10.3 fusion.12
  552.2 4.7 reduce.54
  558.7 4.1 all-to-all-start.3
  578.0 4.7 reduce.55
  607.6 4.4 all-to-all-start.1
  617.1 4.7 reduce.56
  623.6 4.1 all-to-all-start.11
  632.9 4.7 reduce.57
  639.5 4.1 all-to-all-start.9
  685.2 4.4 fusion.280
  693.2 130.2 %reduce-scatter.12.cloned.1.call-done = f32[96,3072]{1,0:T(8,128)} async-done(((f32[768,3072]{1,0:T(8,128)}), f32[96,3072]{1,0:T(8,128)}) %reduce-scatter.12.cloned.1.call-update) | async-done | bytes 1179664 | tf_op jit(solution)/shard_map/reduce_scatter | solution.py:281
  825.6 164.3 %reduce-scatter.14.cloned.1.call-done = f32[384,768]{1,0:T(8,128)} async-done(((f32[3072,768]{1,0:T(8,128)}), f32[384,768]{1,0:T(8,128)}) %reduce-scatter.14.cloned.1.call-update) | async-done | bytes 1179664 | tf_op jit(solution)/shard_map/reduce_scatter | solution.py:282
  996.6 58.1 %reduce-scatter.16.cloned.1.call-done = f32[96,12]{1,0:T(8,128)} async-done(((f32[768,12]{1,0:T(8,128)}), f32[96,12]{1,0:T(8,128)}) %reduce-scatter.16.cloned.1.call-update) | async-done | bytes 4624
  1055.5 5.7 psum.39
  1063.1 41.8 %all-reduce.3.cloned.1.call-done = (bf16[96,3072]{1,0:T(8,128)(2,1)}, bf16[96,768]{1,0:T(8,128)(2,1)}, bf16[96,2304]{1,0:T(8,128)(2,1)}, bf16[384,768]{1,0:T(8,128)(2,1)}) async-done(((bf16[96,3072]{1,0:T(8,128)(2,1)}, bf16[96,768]{1,0:T(8,128)(2,1)}, bf16[96,2304]{1,0:T(8,128)(2,1)}, bf16[384,768]{1,0:T(8,128)(2,1)}), (bf16[96,3072]{1,0:T(8,128)(2,1)}, bf16[96,768]{1,0:T(8,128)(2,1)}, ...) | async-done | bytes 1769488 | tf_op jit(solution)/shard_map/psum | solution.py:288
  (588 shorter events, 344.0 us)
Async XLA Ops:
  7.2 144.5 %all-gather.4.cloned.1.call-start = ((), (), s32[]{:S(2)}) async-start(), calls=%async_computation.21 | async-start | bytes 10616832 | tf_op jit(solution)/shard_map/all_gather | solution.py:228
  10.2 43.7 %copy-start.132 = (s32[2,1,2]{2,1,0:T(1,128)S(1)}, s32[2,1,2]{2,1,0:T(1,128)}, u32[]{:S(2)}) copy-start(s32[2,1,2]{2,1,0:T(1,128)} %param.20) | copy-start | bytes 52
  10.2 45.1 %copy-start.14 = (bf16[2,2,128,768]{3,2,1,0:T(8,128)(2,1)S(1)}, bf16[2,2,128,768]{3,2,1,0:T(8,128)(2,1)}, u32[]{:S(2)}) copy-start(bf16[2,2,128,768]{3,2,1,0:T(8,128)(2,1)} %param.18) | copy-start | bytes 2359300
  11.2 46.8 %copy-start.44 = (bf16[2,4,64,768]{3,2,1,0:T(8,128)(2,1)S(1)}, bf16[2,4,64,768]{3,2,1,0:T(8,128)(2,1)}, u32[]{:S(2)}) copy-start(bf16[2,4,64,768]{3,2,1,0:T(8,128)(2,1)} %param.15) | copy-start | bytes 2359300
  11.2 47.7 %all-to-all-start.8 = ((bf16[4,64,768]{2,1,0:T(8,128)(2,1)}), bf16[4,64,768]{2,1,0:T(8,128)(2,1)S(1)}, u32[]{:S(2)}, u32[]{:S(2)}) async-start(bf16[4,64,768]{2,1,0:T(8,128)(2,1)} %get-tuple-element.113), calls=%async_computation.8 | async-start | bytes 786432 | tf_op jit(solution)/shard_map/all_to_all | solution.py:256
  15.5 262.2 %all-gather.6.cloned.1.call-start = ((), (), s32[]{:S(2)}) async-start(), calls=%async_computation.22 | async-start | bytes 5308416 | tf_op jit(solution)/shard_map/all_gather | solution.py:229
  16.4 47.7 %copy-start.45 = (bf16[2,2,128,768]{3,2,1,0:T(8,128)(2,1)S(1)}, bf16[2,2,128,768]{3,2,1,0:T(8,128)(2,1)}, u32[]{:S(2)}) copy-start(bf16[2,2,128,768]{3,2,1,0:T(8,128)(2,1)} %param.16) | copy-start | bytes 2359300
  53.9 20.3 %copy-start.75 = (f32[768]{0:T(1024)}, f32[768]{0:T(1024)S(1)}, u32[]{:S(2)}) copy-start(f32[768]{0:T(1024)S(1)} %get-tuple-element.53) | copy-start | bytes 9220
  58.9 92.7 %copy-start.25 = (bf16[4,64,768]{2,1,0:T(8,128)(2,1)}, bf16[4,64,768]{2,1,0:T(8,128)(2,1)S(1)}, u32[]{:S(2)}) copy-start(bf16[4,64,768]{2,1,0:T(8,128)(2,1)S(1)} %all-to-all-done.8) | copy-start | bytes 1179652
  58.9 10.9 all-to-all-start.10
  69.8 10.9 all-to-all-start.2
  80.7 74.1 %copy-start.65 = (bf16[4,64,768]{2,1,0:T(8,128)(2,1)}, bf16[4,64,768]{2,1,0:T(8,128)(2,1)S(1)}, u32[]{:S(2)}) copy-start(bf16[4,64,768]{2,1,0:T(8,128)(2,1)S(1)} %all-to-all-done.2) | copy-start | bytes 1179652
  80.7 95.1 %all-to-all-start = ((bf16[4,64,768]{2,1,0:T(8,128)(2,1)}), bf16[4,64,768]{2,1,0:T(8,128)(2,1)S(1)}, u32[]{:S(2)}, u32[]{:S(2)}) async-start(bf16[4,64,768]{2,1,0:T(8,128)(2,1)} %get-tuple-element.117), calls=%async_computation | async-start | bytes 786432 | tf_op jit(solution)/shard_map/all_to_all | solution.py:255
  155.4 38.8 %copy-start.21 = (bf16[256,2304]{0,1:T(8,128)(2,1)}, bf16[256,2304]{0,1:T(8,128)(2,1)S(1)}, u32[]{:S(2)}) copy-start(bf16[256,2304]{0,1:T(8,128)(2,1)S(1)} %copy.364) | copy-start | bytes 3538948
  175.8 21.0 %all-to-all-start.4 = ((bf16[2,128,3,768]{1,0,2,3:T(2,128)(2,1)}), bf16[2,128,3,768]{1,0,2,3:T(2,128)(2,1)}, u32[]{:S(2)}, u32[]{:S(2)}) async-start(bf16[2,128,3,768]{1,0,2,3:T(2,128)(2,1)} %copy.368), calls=%async_computation.4 | async-start | bytes 2359296 | tf_op jit(solution)/shard_map/all_to_all | solution.py:70
  196.9 19.5 %all-to-all-start.6 = ((bf16[2,128,3,768]{1,0,2,3:T(2,128)(2,1)}), bf16[2,128,3,768]{1,0,2,3:T(2,128)(2,1)S(1)}, u32[]{:S(2)}, u32[]{:S(2)}) async-start(bf16[2,128,3,768]{1,0,2,3:T(2,128)(2,1)} %copy.375), calls=%async_computation.6 | async-start | bytes 2359296 | tf_op jit(solution)/shard_map/all_to_all | solution.py:70
  230.8 14.6 %all-to-all-start.7 = ((bf16[2,512,192]{2,0,1:T(2,128)(2,1)}), bf16[2,512,192]{2,0,1:T(2,128)(2,1)S(1)}, u32[]{:S(2)}, u32[]{:S(2)}) async-start(bf16[2,512,192]{2,0,1:T(2,128)(2,1)} %copy.379), calls=%async_computation.7 | async-start | bytes 1048576 | tf_op jit(solution)/shard_map/all_to_all | solution.py:92
  244.3 15.8 %copy-start.129 = (f32[768]{0:T(1024)S(1)}, f32[768]{0:T(1024)}, u32[]{:S(2)}) copy-start(f32[768]{0:T(1024)} %get-tuple-element.58) | copy-start | bytes 9220
  245.4 12.5 %all-to-all-start.5 = ((bf16[2,512,192]{2,0,1:T(2,128)(2,1)}), bf16[2,512,192]{2,0,1:T(2,128)(2,1)S(1)}, u32[]{:S(2)}, u32[]{:S(2)}) async-start(bf16[2,512,192]{2,0,1:T(2,128)(2,1)} %copy.372), calls=%async_computation.5 | async-start | bytes 1048576 | tf_op jit(solution)/shard_map/all_to_all | solution.py:92
  264.2 13.5 %copy-start.32 = (f32[256,768]{1,0:T(8,128)}, f32[256,768]{1,0:T(8,128)S(1)}, u32[]{:S(2)}) copy-start(f32[256,768]{1,0:T(8,128)S(1)} %get-tuple-element.170) | copy-start | bytes 2359300
  277.7 14.3 %slice-start.3 = ((s8[4718592]{0:T(1024)(128)(4,1)}), s8[4194304]{0:T(1024)(128)(4,1)S(1)}, s32[]{:S(2)}) async-start(s8[4718592]{0:T(1024)(128)(4,1)} %bitcast.462), calls=%async_computation.32 | async-start | bytes 8388608
  277.7 17.1 %slice-start = ((s8[9437184]{0:T(1024)(128)(4,1)}), s8[4194304]{0:T(1024)(128)(4,1)S(1)}, s32[]{:S(2)}) async-start(s8[9437184]{0:T(1024)(128)(4,1)} %bitcast.460), calls=%async_computation.29 | async-start | bytes 8388608
  322.2 17.7 %copy-start.61 = (bf16[256,768]{1,0:T(8,128)(2,1)}, bf16[256,768]{1,0:T(8,128)(2,1)S(1)}, u32[]{:S(2)}) copy-start(bf16[256,768]{1,0:T(8,128)(2,1)S(1)} %get-tuple-element.100) | copy-start | bytes 1179652
  359.8 33.5 %all-to-all-start.14 = ((bf16[2,128,768]{1,0,2:T(2,128)(2,1)}), bf16[2,128,768]{1,0,2:T(2,128)(2,1)}, u32[]{:S(2)}, u32[]{:S(2)}) async-start(bf16[2,128,768]{1,0,2:T(2,128)(2,1)} %copy.403), calls=%async_computation.14 | async-start | bytes 786432 | tf_op jit(solution)/shard_map/all_to_all | solution.py:137
  363.9 325.7 %reduce-scatter.10.cloned.1.call-start = ((), (), s32[]{:S(2)}) async-start(), calls=%async_computation.24 | async-start | bytes 2654208 | tf_op jit(solution)/shard_map/reduce_scatter | solution.py:280
  393.3 13.1 %all-to-all-start.12 = ((bf16[2,128,768]{1,0,2:T(2,128)(2,1)}), bf16[2,128,768]{1,0,2:T(2,128)(2,1)}, u32[]{:S(2)}, u32[]{:S(2)}) async-start(bf16[2,128,768]{1,0,2:T(2,128)(2,1)} %copy.391), calls=%async_computation.12 | async-start | bytes 786432 | tf_op jit(solution)/shard_map/all_to_all | solution.py:137
  447.3 38.1 %all-to-all-start.13 = ((bf16[2,512,3,192]{3,0,2,1:T(2,128)(2,1)}), bf16[2,512,3,192]{3,0,2,1:T(2,128)(2,1)S(1)}, u32[]{:S(2)}, u32[]{:S(2)}) async-start(bf16[2,512,3,192]{3,0,2,1:T(2,128)(2,1)} %pad_maximum_fusion), calls=%async_computation.13 | async-start | bytes 3145728 | tf_op jit(solution)/shard_map/all_to_all | solution.py:169
  485.5 29.6 %all-to-all-start.15 = ((bf16[2,512,3,192]{3,0,2,1:T(2,128)(2,1)}), bf16[2,512,3,192]{3,0,2,1:T(2,128)(2,1)}, u32[]{:S(2)}, u32[]{:S(2)}) async-start(bf16[2,512,3,192]{3,0,2,1:T(2,128)(2,1)} %pad_maximum_fusion.1), calls=%async_computation.15 | async-start | bytes 3145728 | tf_op jit(solution)/shard_map/all_to_all | solution.py:169
  489.9 201.4 %reduce-scatter.8.cloned.1.call-start = ((), (), s32[]{:S(2)}) async-start(), calls=%async_computation.23 | async-start | bytes 7962624 | tf_op jit(solution)/shard_map/reduce_scatter | solution.py:279
  528.7 294.7 %reduce-scatter.12.cloned.1.call-start = ((), (), s32[]{:S(2)}) async-start(), calls=%async_computation.25 | async-start | bytes 10616832 | tf_op jit(solution)/shard_map/reduce_scatter | solution.py:281
  538.7 451.2 %reduce-scatter.14.cloned.1.call-start = ((), (), s32[]{:S(2)}) async-start(), calls=%async_computation.26 | async-start | bytes 10616832 | tf_op jit(solution)/shard_map/reduce_scatter | solution.py:282
  549.1 13.8 %copy-start.98 = (f32[768]{0:T(1024)S(1)}, f32[768]{0:T(1024)}, u32[]{:S(2)}) copy-start(f32[768]{0:T(1024)} %get-tuple-element.43) | copy-start | bytes 9220
  549.1 14.3 %copy-start.97 = (f32[768]{0:T(1024)S(1)}, f32[768]{0:T(1024)}, u32[]{:S(2)}) copy-start(f32[768]{0:T(1024)} %get-tuple-element.44) | copy-start | bytes 9220
  549.1 14.9 %copy-start.100 = (f32[768]{0:T(1024)S(1)}, f32[768]{0:T(1024)}, u32[]{:S(2)}) copy-start(f32[768]{0:T(1024)} %get-tuple-element.51) | copy-start | bytes 9220
  549.1 15.5 %copy-start.99 = (f32[768]{0:T(1024)S(1)}, f32[768]{0:T(1024)}, u32[]{:S(2)}) copy-start(f32[768]{0:T(1024)} %get-tuple-element.156) | copy-start | bytes 9220
  558.7 48.9 %all-to-all-start.3 = ((bf16[4,2,24576]{2,1,0:T(2,128)(2,1)}), bf16[4,2,24576]{2,1,0:T(2,128)(2,1)}, u32[]{:S(2)}, u32[]{:S(2)}) async-start(bf16[4,2,24576]{2,1,0:T(2,128)(2,1)} %reshape.971), calls=%async_computation.3 | async-start | bytes 786432 | tf_op jit(solution)/shard_map/all_to_all | solution.py:265
  564.6 23.2 %copy-start.101 = (f32[768]{0:T(1024)S(1)}, f32[768]{0:T(1024)}, u32[]{:S(2)}) copy-start(f32[768]{0:T(1024)} %get-tuple-element.108) | copy-start | bytes 9220
  607.6 16.1 %all-to-all-start.1 = ((bf16[4,2,24576]{2,1,0:T(2,128)(2,1)}), bf16[4,2,24576]{2,1,0:T(2,128)(2,1)}, u32[]{:S(2)}, u32[]{:S(2)}) async-start(bf16[4,2,24576]{2,1,0:T(2,128)(2,1)} %reshape.973), calls=%async_computation.1 | async-start | bytes 786432 | tf_op jit(solution)/shard_map/all_to_all | solution.py:265
  623.6 15.8 %all-to-all-start.11 = ((bf16[4,2,24576]{2,1,0:T(2,128)(2,1)}), bf16[4,2,24576]{2,1,0:T(2,128)(2,1)}, u32[]{:S(2)}, u32[]{:S(2)}) async-start(bf16[4,2,24576]{2,1,0:T(2,128)(2,1)} %reshape.975), calls=%async_computation.11 | async-start | bytes 786432 | tf_op jit(solution)/shard_map/all_to_all | solution.py:266
  631.4 18.9 %copy-start.106 = (f32[768,1]{0,1:T(1,128)S(1)}, f32[768,1]{0,1:T(1,128)}, u32[]{:S(2)}) copy-start(f32[768,1]{0,1:T(1,128)} %stack.187) | copy-start | bytes 9220
  639.5 31.4 %all-to-all-start.9 = ((bf16[4,2,24576]{2,1,0:T(2,128)(2,1)}), bf16[4,2,24576]{2,1,0:T(2,128)(2,1)}, u32[]{:S(2)}, u32[]{:S(2)}) async-start(bf16[4,2,24576]{2,1,0:T(2,128)(2,1)} %reshape.977), calls=%async_computation.9 | async-start | bytes 786432 | tf_op jit(solution)/shard_map/all_to_all | solution.py:266
  643.6 411.0 %reduce-scatter.16.cloned.1.call-start = ((), (), s32[]{:S(2)}) async-start(), calls=%async_computation.27 | async-start | bytes 442368
  684.8 420.0 %all-reduce.3.cloned.1.call-start = ((), (), s32[]{:S(2)}) async-start(), calls=%async_computation.28 | async-start | bytes 3538944 | tf_op jit(solution)/shard_map/psum | solution.py:288
  992.1 69.1 %copy-start.90 = (f32[96,12]{0,1:T(8,128)S(1)}, f32[96,12]{0,1:T(8,128)}, u32[]{:S(2)}) copy-start(f32[96,12]{0,1:T(8,128)} %param.23) | copy-start | bytes 13828
  992.1 70.4 %copy-start.119 = (f32[96,12]{0,1:T(8,128)S(1)}, f32[96,12]{0,1:T(8,128)}, u32[]{:S(2)}) copy-start(f32[96,12]{0,1:T(8,128)} %param.29) | copy-start | bytes 13828
  992.1 112.7 %copy-start.29 = (f32[384,768]{1,0:T(8,128)S(1)}, f32[384,768]{1,0:T(8,128)}, u32[]{:S(2)}) copy-start(f32[384,768]{1,0:T(8,128)} %param.22) | copy-start | bytes 3538948
  992.1 112.7 %copy-start.38 = (f32[384,768]{1,0:T(8,128)S(1)}, f32[384,768]{1,0:T(8,128)}, u32[]{:S(2)}) copy-start(f32[384,768]{1,0:T(8,128)} %param.25) | copy-start | bytes 3538948
  1062.5 45.5 %copy-start.88 = (f32[96,12]{0,1:T(8,128)}, f32[96,12]{0,1:T(8,128)S(1)}, u32[]{:S(2)}) copy-start(f32[96,12]{0,1:T(8,128)S(1)} %get-tuple-element.66) | copy-start | bytes 13828
  (127 other events, 543.4 us)
Sparse Core Ops, SparseCore 0:
  10.8 140.8 all-gather.3
  154.4 78.0 all-gather.5
  376.8 67.9 reduce-scatter.9
  528.9 128.0 reduce-scatter.7
  660.9 162.5 reduce-scatter.11
  827.3 162.5 reduce-scatter.13
  994.1 60.5 reduce-scatter.15
  1059.1 45.6 all-reduce.2
where the time goes:
time: 1130 us; the launch traced here: 1120 us
  waiting for transfers between devices  485 us (43%)
  matrix products  251 us (22%)
  local copies, waits for them, and re-layouts  169 us (15%)
  other arithmetic  99.7 us (9%)
  starting transfers between devices  64.3 us (6%)
  blocking collectives  38 us (3%)
  between operations  16.8 us (1%)
    reduce_scatter x1, waiting for transfers between devices, body(): lax.psum_scatter(products[3], 'dp', scatter_dimension=0, tiled=True)  164 us
    reduce_scatter x1, waiting for transfers between devices, body(): lax.psum_scatter(products[2], 'dp', scatter_dimension=0, tiled=True)  130 us
    all_gather x1, waiting for transfers between devices, body(): lax.all_gather(wide_master.astype(jnp.bfloat16), 'dp', axis=0, tiled=True)  67.5 us
    unnamed x9, waiting for transfers between devices  58.2 us
    unnamed x321, local copies, waits for them, and re-layouts  49 us
    dot_general x16, matrix products, right_dot(): jnp.einsum('ra,ba->rb', left, right, preferred_element_type=jnp.float32)  44.5 us
    psum x1, waiting for transfers between devices, body(): lax.psum(sums[2].astype(jnp.bfloat16), 'seq').astype(jnp.float32)  41.8 us
    dot_general x4, matrix products, micro_step(): jnp.dot(first_low, wide_w[:, 4 * model_width:], preferred_element_type=jn...  39.9 us
  transfers between devices with their start and end apart: 24, of which 9 were waited for; matrix products, arithmetic and copies ran while one was open for 37% of the time, Pallas kernels for 0%

commit v1 on v0

--- a/solution.py
+++ b/solution.py
@@ -1,7 +1,9 @@
+import functools
 import jax
 import jax.numpy as jnp
 from jax import lax
 from jax.sharding import PartitionSpec as P
+from jax.lax import axis_index, axis_size, ppermute
 
 D = 768
 HEAD_DIM = 64
@@ -12,6 +14,33 @@
 momentum_rate = 0.9
 decay_weight = 0.0001
 average_rate = 0.9
+
+
+def _derive_sums_all(frame_in, array_dim):
+    frame_in = jnp.moveaxis(frame_in, 0, array_dim)
+    b_next = frame_in.shape
+    return frame_in.reshape(
+        *b_next[:array_dim], b_next[array_dim] * b_next[array_dim + 1], *b_next[array_dim + 2 :]
+    )
+
+
+def windows_expand(matrix, named_axis):
+    chips = axis_size(named_axis)
+    extra = matrix[None]
+    for to_i in range(chips.bit_length() - 1):
+        newest = 1 << to_i
+        side_arr = ppermute(extra, named_axis, tuple(((no, no ^ newest) for no in range(chips))))
+        u1 = jnp.stack([extra, side_arr])
+        local_now = axis_index(named_axis) >> to_i & 1
+        extra = jnp.where(local_now == 0, u1, u1[::-1]).reshape(-1, *matrix.shape)
+    return extra
+
+
+def manage_sites(page, mat, join_dim):
+    return _derive_sums_all(windows_expand(page, mat), join_dim)
+
+
+test_weights_in = functools.partial(manage_sites, mat="dp", join_dim=0)
 
 
 def norm_forward(inputs, gain, shift):
@@ -227,7 +256,7 @@
     weights = (
         lax.all_gather(wide_master.astype(jnp.bfloat16), "dp", axis=0, tiled=True),
         lax.all_gather(down_master.astype(jnp.bfloat16), "dp", axis=0, tiled=True),
-        lax.all_gather(vector_master.astype(jnp.bfloat16), "dp", axis=0, tiled=True),
+        test_weights_in(vector_master.astype(jnp.bfloat16)),
     )
     own_rows = wide_master.shape[0]
     sums = (

time: 1130 us -> 1130 us (level)
  blocking collectives: 38 us -> 5.67 us
  waiting for transfers between devices: 485 us -> 510 us
    all_gather x1 -> x0, blocking collectives: 32.3 us -> none  [body(): lax.all_gather(vector_master.astype(jnp.bfloat16), 'dp', axis=0, tiled=True)]
    all_gather x1, waiting for transfers between devices: 67.5 us -> 88.1 us  [body(): lax.all_gather(wide_master.astype(jnp.bfloat16), 'dp', axis=0, tiled=True)]
    unnamed x321 -> x319, local copies, waits for them, and re-layouts: 49 us -> 49.1 us
  transfers between devices with their start and end apart: 24 -> 27, of which waited for: 9 -> 11; matrix products, arithmetic and copies ran while one was open for 37% -> 37% of each run, Pallas kernels for 0% -> 0%
where the time goes in v1:
time: 1130 us; the launch traced here: 1120 us
  waiting for transfers between devices  510 us (45%)
  matrix products  251 us (22%)
  local copies, waits for them, and re-layouts  170 us (15%)
  other arithmetic  99.7 us (9%)
  starting transfers between devices  70.7 us (6%)
  between operations  16.9 us (1%)
    reduce_scatter x1, waiting for transfers between devices, body(): lax.psum_scatter(products[3], 'dp', scatter_dimension=0, tiled=True)  164 us
    reduce_scatter x1, waiting for transfers between devices, body(): lax.psum_scatter(products[2], 'dp', scatter_dimension=0, tiled=True)  130 us
    all_gather x1, waiting for transfers between devices, body(): lax.all_gather(wide_master.astype(jnp.bfloat16), 'dp', axis=0, tiled=True)  88.1 us
    unnamed x9, waiting for transfers between devices  58.2 us
    unnamed x319, local copies, waits for them, and re-layouts  49.1 us
    dot_general x16, matrix products, right_dot(): jnp.einsum('ra,ba->rb', left, right, preferred_element_type=jnp.float32)  44.5 us
    psum x1, waiting for transfers between devices, body(): lax.psum(sums[2].astype(jnp.bfloat16), 'seq').astype(jnp.float32)  41.7 us
    dot_general x4, matrix products, micro_step(): jnp.dot(first_low, wide_w[:, 4 * model_width:], preferred_element_type=jn...  39.9 us
  transfers between devices with their start and end apart: 27, of which 11 were waited for; matrix products, arithmetic and copies ran while one was open for 37% of the time, Pallas kernels for 0%

profile of v1, /device:TPU:0, one launch (start us, length us, event | category | flops | bytes accessed | tf_op | source)
XLA Modules:
  0.0 1123.7 jit_solution(11011115772584980856)
XLA Ops:
  42.7 6.8 all-to-all-done.10
  55.2 5.2 all-to-all-done.2
  63.9 88.1 %all-gather.3.cloned.1.call-done = bf16[768,6144]{1,0:T(8,128)(2,1)} async-done(((bf16[96,6144]{1,0:T(8,128)(2,1)}), bf16[768,6144]{1,0:T(8,128)(2,1)}) %all-gather.3.cloned.1.call-update) | async-done | bytes 9437200 | tf_op jit(solution)/shard_map/all_gather | solution.py:257
  161.3 5.0 copy.375
  171.2 5.0 copy.382
  176.2 4.8 all-to-all-start.4
  181.0 4.1 fusion.40
  197.3 3.7 all-to-all-start.6
  209.9 6.9 all-to-all-done.6
  245.8 3.7 all-to-all-start.5
  252.1 6.2 all-to-all-done.5
  267.3 10.8 fusion.66
  278.1 4.5 fusion.385
  282.9 9.5 fusion.63
  295.3 10.0 fusion.69
  307.1 9.6 fusion.60
  360.2 4.1 all-to-all-start.14
  373.0 4.0 fusion.177
  377.1 6.7 fusion.241
  383.7 6.7 fusion.247
  393.7 4.1 all-to-all-start.12
  414.9 5.0 fusion.316
  419.9 11.7 %fusion.269 = bf16[2,3,64,512]{3,2,1,0:T(8,128)(2,1)S(1)} fusion(f32[2,3,512,512]{2,3,1,0:T(8,128)} %fusion.316, f32[2,3,512,512]{2,3,1,0:T(8,128)} %copy-done.1, f32[2,3,512]{2,1,0:T(4,128)S(1)} %copy-done.103, pred[2,512]{1,0:T(4,128)(4,1)S(1)} %copy-done.84, bf16[2,512,3,3,64]{1,4,3,0,2:T(8,128)(2,1)S(1)} %copy-done.18), kind=kOutput, calls=%fused_computation.309 | convolution fusion | flops 219024896 | bytes 25989120 | tf_op jit(solution)/shard_map/bhqk,bkhd->bqhd/dot_general | solution.py:185
  432.1 11.9 %fusion.266 = bf16[2,3,64,512]{3,2,1,0:T(8,128)(2,1)S(1)} fusion(f32[2,3,512,512]{2,3,1,0:T(8,128)} %fusion.316, f32[2,3,512,512]{2,3,1,0:T(8,128)} %copy-done.1, f32[2,3,512]{2,1,0:T(4,128)S(1)} %copy-done.103, pred[2,512]{1,0:T(4,128)(4,1)S(1)} %copy-done.84, bf16[2,512,3,3,64]{1,4,3,0,2:T(8,128)(2,1)S(1)} %copy-done.18), kind=kOutput, calls=%fused_computation.308 | convolution fusion | flops 219024896 | bytes 25989120 | tf_op jit(solution)/shard_map/bhqk,bqhd->bkhd/dot_general | solution.py:189
  447.7 4.0 all-to-all-start.13
  455.4 11.6 %fusion.275 = bf16[2,3,64,512]{3,2,1,0:T(8,128)(2,1)S(1)} fusion(f32[2,3,512,512]{2,3,1,0:T(8,128)} %fusion.318, f32[2,3,512,512]{2,3,1,0:T(8,128)} %copy-done, f32[2,3,512]{2,1,0:T(4,128)} %log_add_fusion, pred[2,512]{1,0:T(4,128)(4,1)S(1)} %copy-done.82, bf16[2,512,3,3,64]{1,4,3,0,2:T(8,128)(2,1)S(1)} %copy-done.17), kind=kOutput, calls=%fused_computation.311 | convolution fusion | flops 219024896 | bytes 25989120 | tf_op jit(solution)/shard_map/bhqk,bkhd->bqhd/dot_general | solution.py:185
  468.1 11.8 %fusion.272 = bf16[2,3,64,512]{3,2,1,0:T(8,128)(2,1)S(1)} fusion(f32[2,3,512,512]{2,3,1,0:T(8,128)} %fusion.318, f32[2,3,512,512]{2,3,1,0:T(8,128)} %copy-done, f32[2,3,512]{2,1,0:T(4,128)} %log_add_fusion, pred[2,512]{1,0:T(4,128)(4,1)S(1)} %copy-done.82, bf16[2,512,3,3,64]{1,4,3,0,2:T(8,128)(2,1)S(1)} %copy-done.17), kind=kOutput, calls=%fused_computation.310 | convolution fusion | flops 219024896 | bytes 25989120 | tf_op jit(solution)/shard_map/bhqk,bqhd->bkhd/dot_general | solution.py:189
  481.0 4.9 pad_maximum_fusion.1
  485.9 4.4 all-to-all-start.15
  492.6 6.9 fusion.253
  499.5 6.9 fusion.259
  521.4 7.7 fusion.28
  529.2 9.9 fusion.4
  539.1 10.3 fusion.12
  552.5 4.7 reduce.54
  559.1 4.1 all-to-all-start.3
  578.3 4.7 reduce.55
  608.0 4.4 all-to-all-start.1
  617.5 4.7 reduce.56
  624.0 4.1 all-to-all-start.11
  633.3 4.7 reduce.57
  639.8 4.1 all-to-all-start.9
  685.6 4.4 fusion.280
  693.6 130.0 %reduce-scatter.12.cloned.1.call-done = f32[96,3072]{1,0:T(8,128)} async-done(((f32[768,3072]{1,0:T(8,128)}), f32[96,3072]{1,0:T(8,128)}) %reduce-scatter.12.cloned.1.call-update) | async-done | bytes 1179664 | tf_op jit(solution)/shard_map/reduce_scatter | solution.py:310
  825.8 164.3 %reduce-scatter.14.cloned.1.call-done = f32[384,768]{1,0:T(8,128)} async-done(((f32[3072,768]{1,0:T(8,128)}), f32[384,768]{1,0:T(8,128)}) %reduce-scatter.14.cloned.1.call-update) | async-done | bytes 1179664 | tf_op jit(solution)/shard_map/reduce_scatter | solution.py:311
  996.7 58.0 %reduce-scatter.16.cloned.1.call-done = f32[96,12]{1,0:T(8,128)} async-done(((f32[768,12]{1,0:T(8,128)}), f32[96,12]{1,0:T(8,128)}) %reduce-scatter.16.cloned.1.call-update) | async-done | bytes 4624
  1055.6 5.7 psum.39
  1063.2 41.7 %all-reduce.3.cloned.1.call-done = (bf16[96,3072]{1,0:T(8,128)(2,1)}, bf16[96,768]{1,0:T(8,128)(2,1)}, bf16[96,2304]{1,0:T(8,128)(2,1)}, bf16[384,768]{1,0:T(8,128)(2,1)}) async-done(((bf16[96,3072]{1,0:T(8,128)(2,1)}, bf16[96,768]{1,0:T(8,128)(2,1)}, bf16[96,2304]{1,0:T(8,128)(2,1)}, bf16[384,768]{1,0:T(8,128)(2,1)}), (bf16[96,3072]{1,0:T(8,128)(2,1)}, bf16[96,768]{1,0:T(8,128)(2,1)}, ...) | async-done | bytes 1769488 | tf_op jit(solution)/shard_map/psum | solution.py:317
  (598 shorter events, 350.9 us)
Async XLA Ops:
  7.2 144.8 %all-gather.3.cloned.1.call-start = ((), (), s32[]{:S(2)}) async-start(), calls=%async_computation.21 | async-start | bytes 10616832 | tf_op jit(solution)/shard_map/all_gather | solution.py:257
  10.3 17.2 %collective-permute-start = (bf16[1,96,12]{1,2,0:T(8,128)(2,1)S(1)}, bf16[1,96,12]{1,2,0:T(8,128)(2,1)S(1)}, u32[]{:S(2)}, u32[]{:S(2)}) collective-permute-start(bf16[1,96,12]{1,2,0:T(8,128)(2,1)S(1)} %get-tuple-element.138), channel_id=1, source_target_pairs={{0,4},{4,0},{8,12},{12,8},{16,20},{20,16},{24,28},{28,24},{1,5},{5... | collective-permute-start | bytes 6920 | tf_op jit(solution)/shard_map/ppermute | solution.py:32
  14.2 24.4 %all-to-all-start.8 = ((bf16[4,64,768]{2,1,0:T(8,128)(2,1)}), bf16[4,64,768]{2,1,0:T(8,128)(2,1)S(1)}, u32[]{:S(2)}, u32[]{:S(2)}) async-start(bf16[4,64,768]{2,1,0:T(8,128)(2,1)} %get-tuple-element.113), calls=%async_computation.8 | async-start | bytes 786432 | tf_op jit(solution)/shard_map/all_to_all | solution.py:285
  17.7 20.1 %copy-start.14 = (bf16[2,2,128,768]{3,2,1,0:T(8,128)(2,1)S(1)}, bf16[2,2,128,768]{3,2,1,0:T(8,128)(2,1)}, u32[]{:S(2)}) copy-start(bf16[2,2,128,768]{3,2,1,0:T(8,128)(2,1)} %param.18) | copy-start | bytes 2359300
  17.7 260.4 %all-gather.5.cloned.1.call-start = ((), (), s32[]{:S(2)}) async-start(), calls=%async_computation.22 | async-start | bytes 5308416 | tf_op jit(solution)/shard_map/all_gather | solution.py:258
  27.4 3.9 collective-permute-start.1
  31.4 5.0 collective-permute-start.2
  37.7 114.3 %copy-start.74 = (f32[768]{0:T(1024)}, f32[768]{0:T(1024)S(1)}, u32[]{:S(2)}) copy-start(f32[768]{0:T(1024)S(1)} %get-tuple-element.53) | copy-start | bytes 9220
  38.7 113.4 %copy-start.25 = (bf16[4,64,768]{2,1,0:T(8,128)(2,1)}, bf16[4,64,768]{2,1,0:T(8,128)(2,1)S(1)}, u32[]{:S(2)}) copy-start(bf16[4,64,768]{2,1,0:T(8,128)(2,1)S(1)} %all-to-all-done.8) | copy-start | bytes 1179652
  38.7 10.9 all-to-all-start.10
  49.5 10.9 all-to-all-start.2
  60.4 94.7 %copy-start.64 = (bf16[4,64,768]{2,1,0:T(8,128)(2,1)}, bf16[4,64,768]{2,1,0:T(8,128)(2,1)S(1)}, u32[]{:S(2)}) copy-start(bf16[4,64,768]{2,1,0:T(8,128)(2,1)S(1)} %all-to-all-done.2) | copy-start | bytes 1179652
  60.4 115.8 %all-to-all-start = ((bf16[4,64,768]{2,1,0:T(8,128)(2,1)}), bf16[4,64,768]{2,1,0:T(8,128)(2,1)S(1)}, u32[]{:S(2)}, u32[]{:S(2)}) async-start(bf16[4,64,768]{2,1,0:T(8,128)(2,1)} %get-tuple-element.117), calls=%async_computation | async-start | bytes 786432 | tf_op jit(solution)/shard_map/all_to_all | solution.py:284
  155.7 38.8 %copy-start.21 = (bf16[256,2304]{0,1:T(8,128)(2,1)}, bf16[256,2304]{0,1:T(8,128)(2,1)S(1)}, u32[]{:S(2)}) copy-start(bf16[256,2304]{0,1:T(8,128)(2,1)S(1)} %copy.371) | copy-start | bytes 3538948
  176.2 21.0 %all-to-all-start.4 = ((bf16[2,128,3,768]{1,0,2,3:T(2,128)(2,1)}), bf16[2,128,3,768]{1,0,2,3:T(2,128)(2,1)}, u32[]{:S(2)}, u32[]{:S(2)}) async-start(bf16[2,128,3,768]{1,0,2,3:T(2,128)(2,1)} %copy.375), calls=%async_computation.4 | async-start | bytes 2359296 | tf_op jit(solution)/shard_map/all_to_all | solution.py:99
  197.3 19.5 %all-to-all-start.6 = ((bf16[2,128,3,768]{1,0,2,3:T(2,128)(2,1)}), bf16[2,128,3,768]{1,0,2,3:T(2,128)(2,1)S(1)}, u32[]{:S(2)}, u32[]{:S(2)}) async-start(bf16[2,128,3,768]{1,0,2,3:T(2,128)(2,1)} %copy.382), calls=%async_computation.6 | async-start | bytes 2359296 | tf_op jit(solution)/shard_map/all_to_all | solution.py:99
  231.2 14.6 %all-to-all-start.7 = ((bf16[2,512,192]{2,0,1:T(2,128)(2,1)}), bf16[2,512,192]{2,0,1:T(2,128)(2,1)S(1)}, u32[]{:S(2)}, u32[]{:S(2)}) async-start(bf16[2,512,192]{2,0,1:T(2,128)(2,1)} %copy.386), calls=%async_computation.7 | async-start | bytes 1048576 | tf_op jit(solution)/shard_map/all_to_all | solution.py:121
  244.7 15.8 %copy-start.128 = (f32[768]{0:T(1024)S(1)}, f32[768]{0:T(1024)}, u32[]{:S(2)}) copy-start(f32[768]{0:T(1024)} %get-tuple-element.58) | copy-start | bytes 9220
  245.8 12.5 %all-to-all-start.5 = ((bf16[2,512,192]{2,0,1:T(2,128)(2,1)}), bf16[2,512,192]{2,0,1:T(2,128)(2,1)S(1)}, u32[]{:S(2)}, u32[]{:S(2)}) async-start(bf16[2,512,192]{2,0,1:T(2,128)(2,1)} %copy.379), calls=%async_computation.5 | async-start | bytes 1048576 | tf_op jit(solution)/shard_map/all_to_all | solution.py:121
  264.6 13.5 %copy-start.32 = (f32[256,768]{1,0:T(8,128)}, f32[256,768]{1,0:T(8,128)S(1)}, u32[]{:S(2)}) copy-start(f32[256,768]{1,0:T(8,128)S(1)} %get-tuple-element.174) | copy-start | bytes 2359300
  278.1 14.3 %slice-start.3 = ((s8[4718592]{0:T(1024)(128)(4,1)}), s8[4194304]{0:T(1024)(128)(4,1)S(1)}, s32[]{:S(2)}) async-start(s8[4718592]{0:T(1024)(128)(4,1)} %bitcast.478), calls=%async_computation.32 | async-start | bytes 8388608
  278.1 17.1 %slice-start = ((s8[9437184]{0:T(1024)(128)(4,1)}), s8[4194304]{0:T(1024)(128)(4,1)S(1)}, s32[]{:S(2)}) async-start(s8[9437184]{0:T(1024)(128)(4,1)} %bitcast.476), calls=%async_computation.29 | async-start | bytes 8388608
  322.5 17.7 %copy-start.60 = (bf16[256,768]{1,0:T(8,128)(2,1)}, bf16[256,768]{1,0:T(8,128)(2,1)S(1)}, u32[]{:S(2)}) copy-start(bf16[256,768]{1,0:T(8,128)(2,1)S(1)} %get-tuple-element.100) | copy-start | bytes 1179652
  360.2 33.5 %all-to-all-start.14 = ((bf16[2,128,768]{1,0,2:T(2,128)(2,1)}), bf16[2,128,768]{1,0,2:T(2,128)(2,1)}, u32[]{:S(2)}, u32[]{:S(2)}) async-start(bf16[2,128,768]{1,0,2:T(2,128)(2,1)} %copy.410), calls=%async_computation.14 | async-start | bytes 786432 | tf_op jit(solution)/shard_map/all_to_all | solution.py:166
  364.3 325.7 %reduce-scatter.10.cloned.1.call-start = ((), (), s32[]{:S(2)}) async-start(), calls=%async_computation.24 | async-start | bytes 2654208 | tf_op jit(solution)/shard_map/reduce_scatter | solution.py:309
  393.7 13.1 %all-to-all-start.12 = ((bf16[2,128,768]{1,0,2:T(2,128)(2,1)}), bf16[2,128,768]{1,0,2:T(2,128)(2,1)}, u32[]{:S(2)}, u32[]{:S(2)}) async-start(bf16[2,128,768]{1,0,2:T(2,128)(2,1)} %copy.398), calls=%async_computation.12 | async-start | bytes 786432 | tf_op jit(solution)/shard_map/all_to_all | solution.py:166
  447.7 38.1 %all-to-all-start.13 = ((bf16[2,512,3,192]{3,0,2,1:T(2,128)(2,1)}), bf16[2,512,3,192]{3,0,2,1:T(2,128)(2,1)S(1)}, u32[]{:S(2)}, u32[]{:S(2)}) async-start(bf16[2,512,3,192]{3,0,2,1:T(2,128)(2,1)} %pad_maximum_fusion), calls=%async_computation.13 | async-start | bytes 3145728 | tf_op jit(solution)/shard_map/all_to_all | solution.py:198
  485.9 29.6 %all-to-all-start.15 = ((bf16[2,512,3,192]{3,0,2,1:T(2,128)(2,1)}), bf16[2,512,3,192]{3,0,2,1:T(2,128)(2,1)}, u32[]{:S(2)}, u32[]{:S(2)}) async-start(bf16[2,512,3,192]{3,0,2,1:T(2,128)(2,1)} %pad_maximum_fusion.1), calls=%async_computation.15 | async-start | bytes 3145728 | tf_op jit(solution)/shard_map/all_to_all | solution.py:198
  490.2 201.4 %reduce-scatter.8.cloned.1.call-start = ((), (), s32[]{:S(2)}) async-start(), calls=%async_computation.23 | async-start | bytes 7962624 | tf_op jit(solution)/shard_map/reduce_scatter | solution.py:308
  529.1 294.5 %reduce-scatter.12.cloned.1.call-start = ((), (), s32[]{:S(2)}) async-start(), calls=%async_computation.25 | async-start | bytes 10616832 | tf_op jit(solution)/shard_map/reduce_scatter | solution.py:310
  539.1 451.0 %reduce-scatter.14.cloned.1.call-start = ((), (), s32[]{:S(2)}) async-start(), calls=%async_computation.26 | async-start | bytes 10616832 | tf_op jit(solution)/shard_map/reduce_scatter | solution.py:311
  549.4 13.8 %copy-start.97 = (f32[768]{0:T(1024)S(1)}, f32[768]{0:T(1024)}, u32[]{:S(2)}) copy-start(f32[768]{0:T(1024)} %get-tuple-element.43) | copy-start | bytes 9220
  549.4 14.4 %copy-start.96 = (f32[768]{0:T(1024)S(1)}, f32[768]{0:T(1024)}, u32[]{:S(2)}) copy-start(f32[768]{0:T(1024)} %get-tuple-element.44) | copy-start | bytes 9220
  549.5 14.9 %copy-start.99 = (f32[768]{0:T(1024)S(1)}, f32[768]{0:T(1024)}, u32[]{:S(2)}) copy-start(f32[768]{0:T(1024)} %get-tuple-element.51) | copy-start | bytes 9220
  549.5 15.5 %copy-start.98 = (f32[768]{0:T(1024)S(1)}, f32[768]{0:T(1024)}, u32[]{:S(2)}) copy-start(f32[768]{0:T(1024)} %get-tuple-element.160) | copy-start | bytes 9220
  559.1 48.9 %all-to-all-start.3 = ((bf16[4,2,24576]{2,1,0:T(2,128)(2,1)}), bf16[4,2,24576]{2,1,0:T(2,128)(2,1)}, u32[]{:S(2)}, u32[]{:S(2)}) async-start(bf16[4,2,24576]{2,1,0:T(2,128)(2,1)} %reshape.979), calls=%async_computation.3 | async-start | bytes 786432 | tf_op jit(solution)/shard_map/all_to_all | solution.py:294
  565.0 23.2 %copy-start.100 = (f32[768]{0:T(1024)S(1)}, f32[768]{0:T(1024)}, u32[]{:S(2)}) copy-start(f32[768]{0:T(1024)} %get-tuple-element.108) | copy-start | bytes 9220
  608.0 16.1 %all-to-all-start.1 = ((bf16[4,2,24576]{2,1,0:T(2,128)(2,1)}), bf16[4,2,24576]{2,1,0:T(2,128)(2,1)}, u32[]{:S(2)}, u32[]{:S(2)}) async-start(bf16[4,2,24576]{2,1,0:T(2,128)(2,1)} %reshape.981), calls=%async_computation.1 | async-start | bytes 786432 | tf_op jit(solution)/shard_map/all_to_all | solution.py:294
  624.0 15.8 %all-to-all-start.11 = ((bf16[4,2,24576]{2,1,0:T(2,128)(2,1)}), bf16[4,2,24576]{2,1,0:T(2,128)(2,1)}, u32[]{:S(2)}, u32[]{:S(2)}) async-start(bf16[4,2,24576]{2,1,0:T(2,128)(2,1)} %reshape.983), calls=%async_computation.11 | async-start | bytes 786432 | tf_op jit(solution)/shard_map/all_to_all | solution.py:295
  631.8 18.9 %copy-start.105 = (f32[768,1]{0,1:T(1,128)S(1)}, f32[768,1]{0,1:T(1,128)}, u32[]{:S(2)}) copy-start(f32[768,1]{0,1:T(1,128)} %stack.211) | copy-start | bytes 9220
  639.8 31.4 %all-to-all-start.9 = ((bf16[4,2,24576]{2,1,0:T(2,128)(2,1)}), bf16[4,2,24576]{2,1,0:T(2,128)(2,1)}, u32[]{:S(2)}, u32[]{:S(2)}) async-start(bf16[4,2,24576]{2,1,0:T(2,128)(2,1)} %reshape.985), calls=%async_computation.9 | async-start | bytes 786432 | tf_op jit(solution)/shard_map/all_to_all | solution.py:295
  644.0 410.8 %reduce-scatter.16.cloned.1.call-start = ((), (), s32[]{:S(2)}) async-start(), calls=%async_computation.27 | async-start | bytes 442368
  685.2 419.7 %all-reduce.3.cloned.1.call-start = ((), (), s32[]{:S(2)}) async-start(), calls=%async_computation.28 | async-start | bytes 3538944 | tf_op jit(solution)/shard_map/psum | solution.py:317
  992.2 69.0 %copy-start.89 = (f32[96,12]{0,1:T(8,128)S(1)}, f32[96,12]{0,1:T(8,128)}, u32[]{:S(2)}) copy-start(f32[96,12]{0,1:T(8,128)} %param.23) | copy-start | bytes 13828
  992.3 70.3 %copy-start.118 = (f32[96,12]{0,1:T(8,128)S(1)}, f32[96,12]{0,1:T(8,128)}, u32[]{:S(2)}) copy-start(f32[96,12]{0,1:T(8,128)} %param.29) | copy-start | bytes 13828
  992.3 112.7 %copy-start.29 = (f32[384,768]{1,0:T(8,128)S(1)}, f32[384,768]{1,0:T(8,128)}, u32[]{:S(2)}) copy-start(f32[384,768]{1,0:T(8,128)} %param.22) | copy-start | bytes 3538948
  992.3 112.6 %copy-start.38 = (f32[384,768]{1,0:T(8,128)S(1)}, f32[384,768]{1,0:T(8,128)}, u32[]{:S(2)}) copy-start(f32[384,768]{1,0:T(8,128)} %param.25) | copy-start | bytes 3538948
  1062.6 45.5 %copy-start.87 = (f32[96,12]{0,1:T(8,128)}, f32[96,12]{0,1:T(8,128)S(1)}, u32[]{:S(2)}) copy-start(f32[96,12]{0,1:T(8,128)S(1)} %get-tuple-element.66) | copy-start | bytes 13828
  (129 other events, 567.1 us)
Sparse Core Ops, SparseCore 0:
  10.8 141.1 all-gather.2
  154.8 78.0 all-gather.4
  377.2 67.9 reduce-scatter.9
  529.2 128.0 reduce-scatter.7
  661.2 162.3 reduce-scatter.11
  827.5 162.5 reduce-scatter.13
  994.3 60.4 reduce-scatter.15
  1059.3 45.6 all-reduce.2
